TPU v7x, 32 devices: a whole 2x2x4 slice. The times are simulated.
32 devices in a mesh: sub: 8 (over z, x), grp: 4 (over y, core).
Axes of the slice: x: 2, y: 2, z: 4, core: 2. Of those that a mesh axis runs over, the one named last changes fastest.
Arguments:
- loads: float32 [4, 16, 2, 48, 256], P('grp', 'sub'), may hold values from -18 to 18
- inv_schur: bfloat16 [4, 16, 1024, 1024], P('grp', 'sub'), as said below
- schur: bfloat16 [4, 16, 1024, 1024], P('grp', 'sub'), as said below
- coarse_map: bfloat16 [4, 16, 12, 1024], P('grp', 'sub'), may hold values from -0.75 to 0.75
- coarse_inverse: float32 [4, 16, 12, 4, 192], P('grp', 'sub'), as said below
- face_rows: int32 [4, 16, 1024], P('grp', 'sub'), may hold values from 0 to 1023, each once within a row
- face_len: int32 [4, 16, 2], P('grp', 'sub'), may hold values from 64 to 256
Outputs:
- multipliers: float32 [4, 16, 2, 48, 256], P('grp', 'sub')
- residual: float32 [4, 16, 2, 48, 256], P('grp', 'sub')
Inputs may be any that keep to these rules, and one draw needn't show every extreme that they name: `inv_schur`: each subdomain's matrix is symmetric and positive definite. `schur`: each subdomain's matrix is symmetric and positive definite. `coarse_inverse`: seen as a [768, 768] matrix it is symmetric and positive definite. `face_rows`: each subdomain's row is a permutation of 0 to 1023.
All inputs are finite; a program needn't handle non-finite values.
Results may differ from a plain program's by a relative error of at most 0.025.
Values sent between devices are 32-bit elements; how exact they have to be, the bound alone decides.
A program may use at most 128 MiB of HBM per device.

v0:
```python
import jax
import jax.numpy as jnp
from jax import lax
from jax.sharding import PartitionSpec as P

FACE = 256
LOADS = 48
CDOF = 12
ITERS = 3


def shifted(value, axis, steps):
    count = lax.axis_size(axis)
    initial, last = (max(0, -steps), min(count, count - steps))
    return lax.ppermute(value, axis, [(source, source + steps) for source in range(initial, last)])


def passed_along(block, axis, distance):
    devices = range(lax.axis_size(axis))
    route = [((i - distance) % len(devices), i) for i in devices]
    return lax.ppermute(block, axis, route)


def pair_sum(first, second, pattern):
    return jnp.einsum(pattern, first, second, precision=lax.Precision.HIGHEST)


def combine(weights, faces):
    return jnp.einsum("ab,gksat->gksbt", weights, faces, precision=lax.Precision.HIGHEST)


def gram_solve(matrix, right):
    return jax.scipy.linalg.cho_solve((jnp.linalg.cholesky(matrix), True), right)


def to_slots(faces):
    along = faces[0, :, 0]
    beside_all = faces[0, :, 1]
    from_left = shifted(along[1:2], "sub", 1)
    from_left = jnp.concatenate([from_left, along[0:1]], axis=0)
    from_below = passed_along(beside_all, "grp", 1)
    stacked = jnp.stack([-from_left, along, -from_below, beside_all], axis=2)
    return stacked.reshape(stacked.shape[0], stacked.shape[1], -1)


def to_faces(field, live_mask):
    pieces = field.reshape(field.shape[0], field.shape[1], 4, -1)
    from_right = shifted(pieces[0:1, :, 0], "sub", -1)
    neighbour = jnp.concatenate([pieces[1:2, :, 0], from_right], axis=0)
    from_above = passed_along(pieces[:, :, 2], "grp", -1)
    jumps = jnp.stack([pieces[:, :, 1] - neighbour, pieces[:, :, 3] - from_above], axis=1)
    return jumps[None] * live_mask


def body(loads, inv_schur, schur, coarse_map, coarse_inverse, face_rows, face_len):
    slot_rows = face_rows[0]
    permute = jax.vmap(lambda matrix, ordering: matrix[ordering][:, ordering])
    solve_mats = permute(inv_schur[0], slot_rows)
    dirichlet = permute(schur[0], slot_rows)
    coarse_basis = jax.vmap(lambda basis_rows, ordering: basis_rows[:, ordering])(
        coarse_map[0], slot_rows
    )
    own_rows = coarse_inverse[0].reshape(2 * CDOF, coarse_inverse.shape[3], coarse_inverse.shape[4])
    positions = jnp.arange(FACE)
    column = 2 * lax.axis_index("sub") + jnp.arange(2)
    last_column = 2 * lax.axis_size("sub") - 1
    along_live = (positions[None, :] < face_len[0, :, 0:1]) & (column[:, None] < last_column)
    around_live = positions[None, :] < face_len[0, :, 1:2]
    live_mask = jnp.stack([along_live, around_live], axis=1).astype(jnp.float32)[
        None, :, :, None, :
    ]

    def precondition(resid):
        slotted = to_slots(resid)
        smoothed = jnp.einsum(
            "krm,kmn->krn",
            slotted.astype(jnp.bfloat16),
            dirichlet,
            preferred_element_type=jnp.float32,
        )
        filtered = to_faces(smoothed, live_mask)
        product = lax.psum(pair_sum(filtered, resid, "gksat,gksbt->ab"), ("sub", "grp"))
        return (filtered, product)

    residual = loads * live_mask
    multipliers = jnp.zeros_like(residual)
    search, precond_gram = precondition(residual)
    direction = search
    for iteration in range(ITERS):
        operator_slotted = to_slots(direction)
        rounded = operator_slotted.astype(jnp.bfloat16)
        local_part = jnp.einsum(
            "krm,kmn->krn", rounded, solve_mats, preferred_element_type=jnp.float32
        )
        operator_coarse_terms = jnp.einsum(
            "krm,kqm->krq", rounded, coarse_basis, preferred_element_type=jnp.float32
        )
        flat_terms = jnp.transpose(operator_coarse_terms, (1, 0, 2)).reshape(1, LOADS, 2 * CDOF)
        cycle_terms = lax.all_gather(flat_terms, "grp", axis=0, tiled=True)
        solved = jnp.einsum(
            "grx,kgx->rk",
            lax.all_gather(cycle_terms, "sub", axis=2, tiled=True),
            own_rows,
            precision=lax.Precision.HIGHEST,
        )
        corrections = jnp.transpose(solved.reshape(LOADS, 2, CDOF), (1, 0, 2)).astype(jnp.bfloat16)
        response = local_part + jnp.einsum(
            "krq,kqm->krm", corrections, coarse_basis, preferred_element_type=jnp.float32
        )
        image_faces = to_faces(response, live_mask)
        curvature = lax.psum(pair_sum(direction, image_faces, "gksat,gksbt->ab"), ("sub", "grp"))
        image_faces, curvature = (image_faces, curvature)
        step_size = gram_solve(curvature, precond_gram)
        multipliers = multipliers + combine(step_size, direction)
        residual = residual - combine(step_size, image_faces)
        if iteration + 1 < ITERS:
            search, new_gram = precondition(residual)
            conjugate = gram_solve(precond_gram, new_gram)
            direction = search + combine(conjugate, direction)
            precond_gram = new_gram
    return (multipliers, residual)


def solution(mesh):
    in_specs = (
        P("grp", "sub", None, None, None),
        P("grp", "sub", None, None),
        P("grp", "sub", None, None),
        P("grp", "sub", None, None),
        P("grp", "sub", None, None, None),
        P("grp", "sub", None),
        P("grp", "sub", None),
    )
    out_specs = (P("grp", "sub", None, None, None), P("grp", "sub", None, None, None))
    return jax.shard_map(body, mesh=mesh, in_specs=in_specs, out_specs=out_specs, check_vma=False)
```

profile of v0, /device:TPU:0, one launch (start us, length us, event | category | flops | bytes accessed | tf_op | source)
XLA Modules:
  0.0 657.6 jit_solution(1124318638356162383)
XLA Ops:
  2.7 4.8 collective-permute-start
  8.4 41.9 %gather_fusion = bf16[2048,1024]{1,0:T(8,128)(2,1)} fusion(bf16[2,1024,1024]{2,1,0:T(8,128)(2,1)} %bitcast.533, s32[2048]{0:T(1024)S(1)} %bitcast.528), kind=kCustom, calls=%fused_computation | custom fusion | bytes 8404992 | tf_op jit(solution)/shard_map/vmap()/gather | solution.py:57
  50.3 6.2 copy.171
  56.6 40.3 %gather_fusion.1 = bf16[2048,1024]{1,0:T(8,128)(2,1)} fusion(bf16[2,1024,1024]{1,2,0:T(8,128)(2,1)} %copy.171, s32[2048]{0:T(1024)S(1)} %bitcast.529), kind=kCustom, calls=%fused_computation.1 | custom fusion | bytes 8404992 | tf_op jit(solution)/shard_map/vmap()/gather | solution.py:57
  96.9 42.0 %gather_fusion.2 = bf16[2048,1024]{1,0:T(8,128)(2,1)} fusion(bf16[2,1024,1024]{2,1,0:T(8,128)(2,1)} %bitcast.534, s32[2048]{0:T(1024)S(1)} %bitcast.530), kind=kCustom, calls=%fused_computation.2 | custom fusion | bytes 8404992 | tf_op jit(solution)/shard_map/vmap()/gather | solution.py:57
  138.9 6.2 copy.182
  145.2 40.4 %gather_fusion.3 = bf16[2048,1024]{1,0:T(8,128)(2,1)} fusion(bf16[2,1024,1024]{1,2,0:T(8,128)(2,1)} %copy.182, s32[2048]{0:T(1024)S(1)} %bitcast.531), kind=kCustom, calls=%fused_computation.3 | custom fusion | bytes 8404992 | tf_op jit(solution)/shard_map/vmap()/gather | solution.py:57
  185.9 11.1 %gather_fusion.4 = bf16[2048,12]{1,0:T(8,128)(2,1)S(1)} fusion(bf16[2,12,1024]{1,2,0:T(8,128)(2,1)S(1)} %bitcast.549, s32[2048]{0:T(1024)S(1)} %bitcast.532), kind=kCustom, calls=%fused_computation.4 | custom fusion | bytes 114688 | tf_op jit(solution)/shard_map/vmap()/gather | solution.py:60
  197.2 3.6 fusion.124
  204.7 2.6 collective-permute-done.2
  207.4 4.6 collective-permute-start.4
  217.9 5.2 all_gather.18
  223.2 31.1 %all_gather.19 = f32[4,48,192]{1,2,0:T(8,128)S(1)} all-gather(f32[4,48,24]{1,2,0:T(8,128)S(1)} %all_gather.18), channel_id=1, replica_groups=mesh['sub'=8,'grp'=4] {'sub'}, dimensions={2}, use_global_device_ids=true | all-gather | bytes 165888 | tf_op jit(solution)/shard_map/all_gather | solution.py:102
  257.1 4.2 collective-permute-done.6
  262.0 38.3 %all-reduce = (f32[48,48]{0,1:T(8,128)S(1)}, f32[48,48]{0,1:T(8,128)S(1)}) all-reduce(f32[48,48]{0,1:T(8,128)S(1)} %convolution_bitcast_fusion.14, f32[48,48]{0,1:T(8,128)S(1)} %convolution_bitcast_fusion.15), channel_id=1, replica_groups=mesh['sub'=8,'grp'=4] {'sub','grp'}, use_global_device_ids=true, to_apply=%region_3.5 | all-reduce | flops 4608 | bytes 36864 | tf_op jit(solution)/shard_map/psum | solution.py:82
  300.4 4.4 cholesky.89
  306.1 3.7 custom-call.21
  311.0 4.1 collective-permute-start.8
  315.2 4.4 cholesky.100
  320.9 3.7 custom-call.22
  324.7 3.6 fusion.126
  331.9 2.6 collective-permute-done.10
  335.0 41.7 %psum.44 = f32[48,48]{0,1:T(8,128)S(1)} all-reduce(f32[48,48]{0,1:T(8,128)S(1)} %convolution_bitcast_fusion.13), channel_id=1, replica_groups=mesh['sub'=8,'grp'=4] {'sub','grp'}, use_global_device_ids=true, to_apply=%region_4.0 | all-reduce | flops 2304 | bytes 18432 | tf_op jit(solution)/shard_map/psum | solution.py:82
  377.6 4.4 cholesky.122
  382.7 4.2 collective-permute-start.12
  387.5 3.7 custom-call.24
  391.3 4.0 collective-permute-done.13
  395.6 3.6 fusion.127
  399.2 5.2 all_gather.20
  404.4 31.1 %all_gather.21 = f32[4,48,192]{1,2,0:T(8,128)S(1)} all-gather(f32[4,48,24]{1,2,0:T(8,128)S(1)} %all_gather.20), channel_id=1, replica_groups=mesh['sub'=8,'grp'=4] {'sub'}, dimensions={2}, use_global_device_ids=true | all-gather | bytes 165888 | tf_op jit(solution)/shard_map/all_gather | solution.py:102
  438.4 4.1 collective-permute-done.14
  442.9 37.8 %psum.45 = f32[48,48]{0,1:T(8,128)S(1)} all-reduce(f32[48,48]{0,1:T(8,128)S(1)} %convolution_bitcast_fusion.12), channel_id=1, replica_groups=mesh['sub'=8,'grp'=4] {'sub','grp'}, use_global_device_ids=true, to_apply=%region_5.0 | all-reduce | flops 2304 | bytes 18432 | tf_op jit(solution)/shard_map/psum | solution.py:111
  480.8 4.4 cholesky.111
  486.5 3.7 custom-call.23
  491.0 4.2 collective-permute-start.16
  496.9 2.4 collective-permute-done.17
  499.4 3.6 fusion.128
  504.8 4.4 collective-permute-done.18
  509.6 41.8 %psum.46 = f32[48,48]{1,0:T(8,128)S(1)} all-reduce(f32[48,48]{1,0:T(8,128)S(1)} %convolution_bitcast_fusion.11), channel_id=1, replica_groups=mesh['sub'=8,'grp'=4] {'sub','grp'}, use_global_device_ids=true, to_apply=%region_6.9 | all-reduce | flops 2304 | bytes 18432 | tf_op jit(solution)/shard_map/psum | solution.py:82
  552.2 4.2 collective-permute-start.20
  558.1 2.4 collective-permute-done.21
  560.8 3.6 fusion.129
  564.4 5.2 all_gather.22
  569.7 31.3 %all_gather.23 = f32[4,48,192]{1,2,0:T(8,128)S(1)} all-gather(f32[4,48,24]{1,2,0:T(8,128)S(1)} %all_gather.22), channel_id=1, replica_groups=mesh['sub'=8,'grp'=4] {'sub'}, dimensions={2}, use_global_device_ids=true | all-gather | bytes 165888 | tf_op jit(solution)/shard_map/all_gather | solution.py:102
  603.6 4.3 collective-permute-done.22
  608.3 37.4 %psum.47 = f32[48,48]{0,1:T(8,128)S(1)} all-reduce(f32[48,48]{0,1:T(8,128)S(1)} %convolution_bitcast_fusion.10), channel_id=1, replica_groups=mesh['sub'=8,'grp'=4] {'sub','grp'}, use_global_device_ids=true, to_apply=%region_7.10 | all-reduce | flops 2304 | bytes 18432 | tf_op jit(solution)/shard_map/psum | solution.py:111
  645.7 4.4 cholesky.133
  651.5 3.7 custom-call.25
  (209 shorter events, 45.8 us)
Async XLA Ops:
  0.6 253.6 %copy-start = (f32[1,2,12,4,192]{4,3,2,1,0:T(4,128)S(1)}, f32[1,2,12,4,192]{4,3,2,1,0:T(4,128)}, u32[]{:S(2)}) copy-start(f32[1,2,12,4,192]{4,3,2,1,0:T(4,128)} %param.14) | copy-start | bytes 221188
  2.7 194.4 %collective-permute-start = (f32[1,48,256]{2,1,0:T(8,128)S(1)}, f32[1,48,256]{2,1,0:T(8,128)S(1)}, u32[]{:S(2)}, u32[]{:S(2)}) collective-permute-start(f32[1,48,256]{2,1,0:T(8,128)S(1)} %get-tuple-element.64), channel_id=1, source_target_pairs={{0,4},{4,8},{8,12},{12,16},{16,20},{20,24},{24,28},{1,5},{5,9},{9,... | collective-permute-start | bytes 147464 | tf_op jit(solution)/shard_map/ppermute | solution.py:15
  7.6 189.5 %collective-permute-start.1 = (f32[2,48,256]{2,1,0:T(8,128)S(1)}, f32[2,48,256]{2,1,0:T(8,128)S(1)}, u32[]{:S(2)}, u32[]{:S(2)}) collective-permute-start(f32[2,48,256]{2,1,0:T(8,128)S(1)} %slice_bitcast_fusion.5), channel_id=1, source_target_pairs={{3,0},{0,1},{1,2},{2,3},{7,4},{4,5},{5,6},{6,7},{11,8},{8,9},{9,10... | collective-permute-start | bytes 294920 | tf_op jit(solution)/shard_map/ppermute | solution.py:21
  145.2 40.5 %copy-start.2 = (bf16[1,2,12,1024]{3,1,2,0:T(2,128)(2,1)S(1)}, bf16[1,2,12,1024]{3,1,2,0:T(2,128)(2,1)}, u32[]{:S(2)}) copy-start(bf16[1,2,12,1024]{3,1,2,0:T(2,128)(2,1)} %param.13) | copy-start | bytes 147460
  200.9 15.3 %copy-start.1 = (bf16[2048,1024]{1,0:T(8,128)(2,1)S(1)}, bf16[2048,1024]{1,0:T(8,128)(2,1)}, u32[]{:S(2)}) copy-start(bf16[2048,1024]{1,0:T(8,128)(2,1)} %gather_fusion.3) | copy-start | bytes 12582916
  201.0 6.2 collective-permute-start.2
  202.9 4.4 collective-permute-start.3
  207.4 6.7 %collective-permute-start.4 = (f32[1,48,256]{2,1,0:T(8,128)S(1)}, f32[1,48,256]{2,1,0:T(8,128)S(1)}, u32[]{:S(2)}, u32[]{:S(2)}) collective-permute-start(f32[1,48,256]{2,1,0:T(8,128)S(1)} %get-tuple-element.58), channel_id=1, source_target_pairs={{0,4},{4,8},{8,12},{12,16},{16,20},{20,24},{24,28},{1,5},{5,9},{9,... | collective-permute-start | bytes 147464 | tf_op jit(solution)/shard_map/ppermute | solution.py:15
  212.1 4.1 collective-permute-start.5
  255.3 6.0 collective-permute-start.6
  256.8 4.4 collective-permute-start.7
  311.0 13.6 %collective-permute-start.8 = (f32[1,48,256]{2,1,0:T(8,128)S(1)}, f32[1,48,256]{2,1,0:T(8,128)S(1)}, u32[]{:S(2)}, u32[]{:S(2)}) collective-permute-start(f32[1,48,256]{2,1,0:T(8,128)S(1)} %get-tuple-element.54), channel_id=1, source_target_pairs={{0,4},{4,8},{8,12},{12,16},{16,20},{20,24},{24,28},{1,5},{5,9},{9,... | collective-permute-start | bytes 147464 | tf_op jit(solution)/shard_map/ppermute | solution.py:15
  315.1 9.5 %collective-permute-start.9 = (f32[2,48,256]{2,1,0:T(8,128)S(1)}, f32[2,48,256]{2,1,0:T(8,128)S(1)}, u32[]{:S(2)}, u32[]{:S(2)}) collective-permute-start(f32[2,48,256]{2,1,0:T(8,128)S(1)} %slice_bitcast_fusion.3), channel_id=1, source_target_pairs={{3,0},{0,1},{1,2},{2,3},{7,4},{4,5},{5,6},{6,7},{11,8},{8,9},{9,10... | collective-permute-start | bytes 294920 | tf_op jit(solution)/shard_map/ppermute | solution.py:21
  328.6 6.0 collective-permute-start.10
  330.2 4.4 collective-permute-start.11
  382.7 8.5 %collective-permute-start.12 = (f32[1,48,256]{2,1,0:T(8,128)S(1)}, f32[1,48,256]{2,1,0:T(8,128)S(1)}, u32[]{:S(2)}, u32[]{:S(2)}) collective-permute-start(f32[1,48,256]{2,1,0:T(8,128)S(1)} %get-tuple-element.48), channel_id=1, source_target_pairs={{0,4},{4,8},{8,12},{12,16},{16,20},{20,24},{24,28},{1,5},{5,9},{9,... | collective-permute-start | bytes 147464 | tf_op jit(solution)/shard_map/ppermute | solution.py:15
  391.2 4.1 collective-permute-start.13
  436.5 6.0 collective-permute-start.14
  438.1 4.4 collective-permute-start.15
  491.0 5.9 collective-permute-start.16
  495.2 4.1 collective-permute-start.17
  503.2 6.0 collective-permute-start.18
  504.8 4.5 collective-permute-start.19
  552.2 5.9 collective-permute-start.20
  556.4 4.1 collective-permute-start.21
  601.9 6.0 collective-permute-start.22
  603.5 4.4 collective-permute-start.23
where the time goes:
time: 662 us; the launch traced here: 658 us
  blocking collectives  306 us (46%)
  local copies, waits for them, and re-layouts  193 us (29%)
  other arithmetic  49.2 us (7%)
  starting transfers between devices  39.2 us (6%)
  waiting for transfers between devices  37.4 us (6%)
  matrix products  30.1 us (5%)
    gather x6, local copies, waits for them, and re-layouts, body(): permute = jax.vmap(lambda matrix, ordering: matrix[ordering][:, ordering])  177 us
    psum x3, blocking collectives, precondition(): lax.psum(pair_sum(filtered, resid, 'gksat,gksbt->ab'), ('sub', 'grp'))  122 us
    all_gather x3, blocking collectives, body(): lax.all_gather(cycle_terms, 'sub', axis=2, tiled=True)  93.5 us
    psum x2, blocking collectives, body(): lax.psum(pair_sum(direction, image_faces, 'gksat,gksbt->ab'), ('sub', 'gr...  75.2 us
    ppermute x12, starting transfers between devices, shifted(): lax.ppermute(value, axis, [(source, source + steps) for source in range(i...  34.1 us
    ppermute x12, waiting for transfers between devices, shifted(): lax.ppermute(value, axis, [(source, source + steps) for source in range(i...  26.6 us
    another operation x15, other arithmetic, gram_solve(): jnp.linalg.cholesky(matrix)  25.3 us
    another operation x10, other arithmetic, gram_solve(): jax.scipy.linalg.cho_solve((jnp.linalg.cholesky(matrix), True), right)  21.6 us
  transfers between devices with their start and end apart: 24, of which 13 were waited for; matrix products, arithmetic and copies ran while one was open for 31% of the time, Pallas kernels for 0%

commit v1 on v0

v1 whole, which is shorter than its diff:
```python
import functools

import jax
import jax.numpy as jnp
from jax import lax
from jax.experimental import pallas as pl
from jax.experimental.pallas import tpu as pltpu
from jax.sharding import PartitionSpec as P

FACE = 256
LOADS = 48
CDOF = 12
ITERS = 3
ORDER = 1024
PADQ = 16
HALF = 64
LANES = 128
HIGHEST = lax.Precision.HIGHEST
MESH = pl.DeviceIdType.MESH
F32 = jnp.float32
BF16 = jnp.bfloat16


def dot_nn(a, b, precision=None):
    return lax.dot_general(
        a, b, (((1,), (0,)), ((), ())), precision=precision, preferred_element_type=F32
    )


def dot_nt(a, b, precision=None):
    return lax.dot_general(
        a, b, (((1,), (1,)), ((), ())), precision=precision, preferred_element_type=F32
    )


def widen(block):
    rows, columns = block.shape
    return jnp.concatenate([block, jnp.zeros((rows, LANES - columns), F32)], axis=1)


def pack_gram(gram):
    wide = widen(gram)
    half = LOADS // 2
    return wide[:half] + pltpu.roll(wide[half:], HALF, 1)


def unpack_gram(packed):
    return jnp.concatenate([packed, pltpu.roll(packed, HALF, 1)], axis=0)


def transposed(wide):
    return widen(jnp.transpose(wide)[:LOADS])


def eliminate(matrix, right):
    lane = lax.broadcasted_iota(jnp.int32, (LOADS, LANES), 1)
    row = lax.broadcasted_iota(jnp.int32, (LOADS, LANES), 0)
    symmetric = 0.5 * (matrix + transposed(matrix))
    both = jnp.where(lane < HALF, symmetric, pltpu.roll(right, HALF, 1))
    for k in range(LOADS):
        pivot_row = both[k : k + 1, :]
        scaled = pivot_row * (1.0 / both[k : k + 1, k : k + 1])
        both = jnp.where(row == k, scaled, both - both[:, k : k + 1] * scaled)
    return pltpu.roll(both, HALF, 1)


def kernel(
    n, ng,
    loads, inv_hbm, schur_hbm, cmap, cinv, frow, flen,
    mult_out, res_out,
    amat, qmat, tmat, pt, pcol, basis, field, from_left, from_right, from_above, from_below,
    live, resid, direc, gram_g, gram_s, term_g, part_s, part_r, cin_g, cin_t,
    load_sem, halo_ss, halo_rs, live_ss, live_rs, cin_ss, cin_rs,
    gg_ss, gg_rs, gs_ss, gs_rs, tg_ss, tg_rs, ps_ss, ps_rs,
):
    s = lax.axis_index("sub")
    g = lax.axis_index("grp")
    right, left = lax.rem(s + 1, n), lax.rem(s + n - 1, n)
    above, below = lax.rem(g + 1, ng), lax.rem(g + ng - 1, ng)

    loaded = []
    for index in range(4):
        source = (schur_hbm if index < 2 else inv_hbm).at[index % 2]
        loaded.append(pltpu.make_async_copy(source, amat.at[index], load_sem.at[index]))
        loaded[-1].start()

    barrier = pltpu.get_barrier_semaphore()
    for i in range(1, ng):
        pl.semaphore_signal(
            barrier, inc=1, device_id={"grp": lax.rem(g + i, ng)}, device_id_type=MESH
        )

    def greet(i, carry):
        pl.semaphore_signal(
            barrier, inc=1, device_id={"sub": lax.rem(s + i, n)}, device_id_type=MESH
        )
        return carry

    lax.fori_loop(1, n, greet, 0)

    position = lax.broadcasted_iota(jnp.int32, (8, FACE), 1)
    for k in range(2):
        along = (position < flen[k, 0]) & (2 * s + k < 2 * n - 1)
        around = position < flen[k, 1]
        live[1, k] = jnp.where(along, 1.0, 0.0)
        live[3, k] = jnp.where(around, 1.0, 0.0)
        field[0, 0, k] = jnp.zeros((LOADS, FACE), F32)
        field[0, 2, k] = jnp.zeros((LOADS, FACE), F32)
        field[0, 1, k] = loads[k, 0]
        field[0, 3, k] = loads[k, 1]
    live[0, 1] = live[1, 0]
    cin_g[pl.ds(g, 1)] = cinv[pl.ds(g, 1)]

    sends = []

    def send(src, dst, send_sem, recv_sem, to):
        copy = pltpu.make_async_remote_copy(
            src_ref=src, dst_ref=dst, send_sem=send_sem, recv_sem=recv_sem,
            device_id=to, device_id_type=MESH,
        )
        copy.start()
        sends.append(copy)
        return copy

    def halo_start(r, first=False):
        copies = [
            send(field.at[r, 1, 1], from_left.at[r], halo_ss.at[r, 0], halo_rs.at[r, 0], {"sub": right}),
            send(field.at[r, 3], from_below.at[r], halo_ss.at[r, 1], halo_rs.at[r, 1], {"grp": above}),
        ]
        if not first:
            copies += [
                send(field.at[r, 0, 0], from_right.at[r], halo_ss.at[r, 2], halo_rs.at[r, 2], {"sub": left}),
                send(field.at[r, 2], from_above.at[r], halo_ss.at[r, 3], halo_rs.at[r, 3], {"grp": below}),
            ]
        return copies

    def jumps(r, copies):
        for copy in copies:
            copy.wait_recv()
        first = len(copies) == 2
        pieces = []
        for k in range(2):
            for slot in range(4):
                if slot == 0:
                    other = from_left[r] if k == 0 else field[r, 1, 0]
                elif slot == 1:
                    other = field[r, 0, 1] if k == 0 else (None if first else from_right[r])
                elif slot == 2:
                    other = from_below[r, k]
                else:
                    other = None if first else from_above[r, k]
                mine = field[r, slot, k]
                jump = mine if other is None else mine - other
                pieces.append(jnp.where(live[slot, k, 0:1, :] > 0.5, jump, 0.0))
        return jnp.concatenate(pieces, axis=1)

    def store_field(r, values):
        for k in range(2):
            for slot in range(4):
                field[r, slot, k] = values[k][:, slot * FACE : (slot + 1) * FACE]

    def group_start(buffer, r, ss, rs):
        for i in range(1, ng):
            pltpu.make_async_remote_copy(
                src_ref=buffer.at[r, g], dst_ref=buffer.at[r, g],
                send_sem=ss.at[r], recv_sem=rs.at[r],
                device_id={"grp": lax.rem(g + i, ng)}, device_id_type=MESH,
            ).start()
        whole = pltpu.make_async_remote_copy(
            src_ref=buffer.at[r, pl.ds(0, ng - 1)], dst_ref=buffer.at[r, pl.ds(0, ng - 1)],
            send_sem=ss.at[r], recv_sem=rs.at[r],
            device_id={"grp": above}, device_id_type=MESH,
        )
        sends.append(whole)
        return whole

    def span_start(source, buffer, r, ss, rs, scatter):
        def step(i, carry):
            peer = lax.rem(s + i, n)
            pltpu.make_async_remote_copy(
                src_ref=source.at[r, peer if scatter else s], dst_ref=buffer.at[r, s],
                send_sem=ss.at[r], recv_sem=rs.at[r],
                device_id={"sub": peer}, device_id_type=MESH,
            ).start()
            return carry

        lax.fori_loop(1, n, step, 0)
        whole = pltpu.make_async_remote_copy(
            src_ref=buffer.at[r, pl.ds(0, n - 1)], dst_ref=buffer.at[r, pl.ds(0, n - 1)],
            send_sem=ss.at[r], recv_sem=rs.at[r],
            device_id={"sub": right}, device_id_type=MESH,
        )
        sends.append(whole)
        return whole

    def reduce_start(r, gram):
        gram_g[r, g] = pack_gram(gram)
        return group_start(gram_g, r, gg_ss, gg_rs)

    def reduce_middle(r, whole):
        whole.wait_recv()
        gram_s[r, s] = jnp.sum(gram_g[r], axis=0)
        return span_start(gram_s, gram_s, r, gs_ss, gs_rs, False)

    def reduce_end(r, whole):
        whole.wait_recv()
        return unpack_gram(jnp.sum(gram_s[r], axis=0))

    pl.semaphore_wait(barrier, ng - 1 + n - 1)

    halo = halo_start(0, first=True)
    live_copies = [
        send(live.at[1, 1], live.at[0, 0], live_ss.at[0], live_rs.at[0], {"sub": right}),
        send(live.at[3], live.at[2], live_ss.at[1], live_rs.at[1], {"grp": above}),
    ]
    cin_copies = []
    for i in range(1, ng):
        peer = lax.rem(g + i, ng)
        cin_copies.append(
            send(cinv.at[peer], cin_g.at[g], cin_ss.at[i], cin_rs.at[i], {"grp": peer})
        )

    for k in range(2):
        rows = frow[k : k + 1, :]
        pcol[k] = jnp.transpose(jnp.broadcast_to(rows, (LANES, ORDER)))

        @pl.loop(0, ORDER // FACE)
        def _(i, k=k):
            at = pl.multiple_of(i * FACE, FACE)
            index = lax.broadcasted_iota(jnp.int32, (FACE, ORDER), 0) + at
            pt[k, pl.ds(at, FACE)] = jnp.where(index == frow[k : k + 1, :], 1.0, 0.0).astype(BF16)

    def reorder(index):
        k = index % 2
        loaded[index].wait()

        @pl.loop(0, ORDER // FACE)
        def _(i):
            at = pl.multiple_of(i * FACE, FACE)
            tmat[pl.ds(at, FACE)] = dot_nn(amat[index, pl.ds(at, FACE)], pt[k]).astype(BF16)

        @pl.loop(0, ORDER // FACE)
        def _(i):
            at = pl.multiple_of(i * FACE, FACE)
            block = pcol[k, pl.ds(at, FACE)]
            wide = jnp.concatenate([block] * (ORDER // LANES), axis=1)
            index_of = lax.broadcasted_iota(jnp.int32, (FACE, ORDER), 1)
            pick = jnp.where(index_of == wide, 1.0, 0.0).astype(BF16)
            qmat[index, pl.ds(at, FACE)] = dot_nn(pick, tmat[...]).astype(BF16)

    def apply(base, rounded):
        return [
            dot_nn(rounded[:, k * ORDER : (k + 1) * ORDER], qmat[base + k]) for k in range(2)
        ]

    reorder(0)
    reorder(1)
    for copy in live_copies:
        copy.wait_recv()
    resid[...] = jumps(0, halo)

    def precondition(r, count):
        values = apply(0, resid[...].astype(BF16))
        store_field(r, values)
        halo = halo_start(r)
        gram = dot_nt(jnp.concatenate(values, axis=1), resid[...], HIGHEST)
        return halo, reduce_start(count, gram)

    halo, stage = precondition(1, 0)
    for k in range(2):
        basis[k] = dot_nn(cmap[k], pt[k]).astype(BF16)
    reorder(2)
    stage = reduce_middle(0, stage)
    for copy in cin_copies:
        copy.wait_recv()
    wide = jnp.concatenate(
        [cin_g[group, k] for k in range(2) for group in range(ng)], axis=0
    )
    cin_t[...] = jnp.transpose(wide)
    reorder(3)
    direc[...] = jumps(1, halo)
    precond_gram = reduce_end(0, stage)

    lane = lax.broadcasted_iota(jnp.int32, (LOADS, LANES), 1)
    row = lax.broadcasted_iota(jnp.int32, (LOADS, LANES), 0)
    identity = jnp.where(lane == row, 1.0, 0.0)

    r, count = 2, 1
    for iteration in range(ITERS):
        rounded = direc[...].astype(BF16)
        terms = [
            widen(dot_nt(basis[k], rounded[:, k * ORDER : (k + 1) * ORDER])) for k in range(2)
        ]
        term_g[iteration, g] = terms[0] + pltpu.roll(terms[1], HALF, 1)
        stage = group_start(term_g, iteration, tg_ss, tg_rs)
        values = apply(2, rounded)
        stage.wait_recv()
        gathered = term_g[iteration].reshape(ng * PADQ, LANES)
        stacked = jnp.concatenate([gathered, pltpu.roll(gathered, HALF, 1)], axis=0)
        shares = dot_nn(cin_t[...], stacked, HIGHEST)
        low = lax.broadcasted_iota(jnp.int32, (n * PADQ, LANES), 1) < HALF
        shares = jnp.where(low, shares[: n * PADQ], pltpu.roll(shares[n * PADQ :], HALF, 1))
        part_s[iteration] = shares.reshape(n, PADQ, LANES)
        part_r[iteration, pl.ds(s, 1)] = part_s[iteration, pl.ds(s, 1)]
        stage = span_start(part_s, part_r, iteration, ps_ss, ps_rs, True)
        stage.wait_recv()
        solved = jnp.transpose(jnp.sum(part_r[iteration], axis=0)).astype(BF16)
        values = [
            values[k] + dot_nn(solved[k * HALF : k * HALF + LOADS], basis[k]) for k in range(2)
        ]
        store_field(r, values)
        halo = halo_start(r)
        gram = dot_nt(direc[...], jnp.concatenate(values, axis=1), HIGHEST)
        stage = reduce_start(count, gram)
        stage = reduce_middle(count, stage)
        image = jumps(r, halo)
        curvature = reduce_end(count, stage)
        r, count = r + 1, count + 1
        step_size = jnp.transpose(eliminate(curvature, precond_gram))[:LOADS]
        resid[...] -= dot_nn(step_size, image, HIGHEST)
        more = iteration + 1 < ITERS
        if more:
            halo, stage = precondition(r, count)
        for k in range(2):
            for side in range(2):
                at = k * ORDER + (2 * side + 1) * FACE
                part = dot_nn(step_size, direc[:, at : at + FACE], HIGHEST)
                if iteration > 0:
                    part = mult_out[k, side] + part
                mult_out[k, side] = part
        if more:
            stage = reduce_middle(count, stage)
            inverse = eliminate(precond_gram, identity)
            search = jumps(r, halo)
            new_gram = reduce_end(count, stage)
            conjugate = dot_nn(inverse[:, :LOADS], new_gram, HIGHEST)
            weights = jnp.transpose(conjugate)[:LOADS]
            direc[...] = search + dot_nn(weights, direc[...], HIGHEST)
            precond_gram = new_gram
            r, count = r + 1, count + 1

    for k in range(2):
        for side in range(2):
            at = k * ORDER + (2 * side + 1) * FACE
            res_out[k, side] = resid[:, at : at + FACE]
    for copy in sends:
        copy.wait_send()


def body(n, ng, loads, inv_schur, schur, coarse_map, coarse_inverse, face_rows, face_len):
    basis_rows = jnp.pad(coarse_map[0], ((0, 0), (0, PADQ - CDOF), (0, 0)))
    own = coarse_inverse[0].reshape(2, CDOF, ng, n, 2, CDOF)
    own = jnp.transpose(own, (2, 0, 1, 4, 3, 5))
    pad = PADQ - CDOF
    own = jnp.pad(own, ((0, 0), (0, 0), (0, pad), (0, 0), (0, 0), (0, pad)))
    own = own.reshape(ng, 2, PADQ, 2 * n * PADQ)

    rounds, grams = 2 * ITERS + 1, 2 * ITERS
    vmem, dma = pltpu.VMEM, pltpu.SemaphoreType.DMA
    faces = jax.ShapeDtypeStruct((2, 2, LOADS, FACE), F32)
    in_vmem = pl.BlockSpec(memory_space=pltpu.VMEM)
    in_hbm = pl.BlockSpec(memory_space=pl.ANY)
    multipliers, residual = pl.pallas_call(
        functools.partial(kernel, n, ng),
        out_shape=(faces, faces),
        in_specs=[
            in_vmem, in_hbm, in_hbm, in_vmem, in_vmem, in_vmem,
            pl.BlockSpec(memory_space=pltpu.SMEM),
        ],
        out_specs=(in_vmem, in_vmem),
        scratch_shapes=[
            vmem((4, ORDER, ORDER), BF16),
            vmem((4, ORDER, ORDER), BF16),
            vmem((ORDER, ORDER), BF16),
            vmem((2, ORDER, ORDER), BF16),
            vmem((2, ORDER, LANES), jnp.int32),
            vmem((2, PADQ, ORDER), BF16),
            vmem((rounds, 4, 2, LOADS, FACE), F32),
            vmem((rounds, LOADS, FACE), F32),
            vmem((rounds, LOADS, FACE), F32),
            vmem((rounds, 2, LOADS, FACE), F32),
            vmem((rounds, 2, LOADS, FACE), F32),
            vmem((4, 2, 8, FACE), F32),
            vmem((LOADS, 2 * ORDER), F32),
            vmem((LOADS, 2 * ORDER), F32),
            vmem((grams, ng, LOADS // 2, LANES), F32),
            vmem((grams, n, LOADS // 2, LANES), F32),
            vmem((ITERS, ng, PADQ, LANES), F32),
            vmem((ITERS, n, PADQ, LANES), F32),
            vmem((ITERS, n, PADQ, LANES), F32),
            vmem((ng, 2, PADQ, 2 * n * PADQ), F32),
            vmem((2 * n * PADQ, 2 * ng * PADQ), F32),
            dma((4,)),
            dma((rounds, 4)), dma((rounds, 4)),
            dma((2,)), dma((2,)),
            dma((ng,)), dma((ng,)),
            dma((grams,)), dma((grams,)),
            dma((grams,)), dma((grams,)),
            dma((ITERS,)), dma((ITERS,)),
            dma((ITERS,)), dma((ITERS,)),
        ],
        compiler_params=pltpu.CompilerParams(
            collective_id=0, has_side_effects=True, vmem_limit_bytes=56 * 1024 * 1024
        ),
    )(loads[0], inv_schur[0], schur[0], basis_rows, own, face_rows[0], face_len[0])
    return multipliers[None], residual[None]


def solution(mesh):
    in_specs = (
        P("grp", "sub", None, None, None),
        P("grp", "sub", None, None),
        P("grp", "sub", None, None),
        P("grp", "sub", None, None),
        P("grp", "sub", None, None, None),
        P("grp", "sub", None),
        P("grp", "sub", None),
    )
    out_specs = (P("grp", "sub", None, None, None), P("grp", "sub", None, None, None))
    run = functools.partial(body, mesh.shape["sub"], mesh.shape["grp"])
    return jax.shard_map(run, mesh=mesh, in_specs=in_specs, out_specs=out_specs, check_vma=False)
```

time: 662 us -> 128 us (0.19)
  blocking collectives: 306 us -> 0 us
  local copies, waits for them, and re-layouts: 193 us -> 7.23 us
  Pallas kernels: 0 us -> 120 us
  other arithmetic: 49.2 us -> 0 us
  starting transfers between devices: 39.2 us -> 0 us
  waiting for transfers between devices: 37.4 us -> 0 us
  matrix products: 30.1 us -> 0 us
    psum x5 -> x0, blocking collectives: 197 us -> none  [the longest x3 122 us: precondition(): lax.psum(pair_sum(filtered, resid, 'gksat,gksbt->ab'), ('sub', 'grp'))]
    gather x7 -> x0, local copies, waits for them, and re-layouts: 188 us -> none  [the longest x6 177 us: body(): permute = jax.vmap(lambda matrix, ordering: matrix[ordering][:, ordering])]
    pallas_call x0 -> x1, Pallas kernels: none -> 120 us  [body(): pl.pallas_call(functools.partial(kernel, n, ng), out_shape=(faces, faces)...]
    all_gather x6 -> x0, blocking collectives: 109 us -> none  [the longest x3 93.5 us: body(): lax.all_gather(cycle_terms, 'sub', axis=2, tiled=True)]
    another operation x46 -> x0, other arithmetic: 47.1 us -> none  [the longest x15 25.3 us: gram_solve(): jnp.linalg.cholesky(matrix)]
    ppermute x24 -> x0, starting transfers between devices: 39.2 us -> none  [the longest x12 34.1 us: shifted(): lax.ppermute(value, axis, [(source, source + steps) for source in range(i...]
    ppermute x24 -> x0, waiting for transfers between devices: 37.4 us -> none  [the longest x12 26.6 us: shifted(): lax.ppermute(value, axis, [(source, source + steps) for source in range(i...]
    dot_general x29 -> x0, matrix products: 27.8 us -> none  [the longest x3 10.7 us: precondition(): jnp.einsum('krm,kmn->krn', slotted.astype(jnp.bfloat16), dirichlet, prefe...]
  transfers between devices with their start and end apart: 24 -> 0, of which waited for: 13 -> 0; matrix products, arithmetic and copies ran while one was open for 31% -> 0% of each run, Pallas kernels for 0% -> 0%
where the time goes in v1:
time: 128 us
  Pallas kernels  120 us (94%)
  local copies, waits for them, and re-layouts  7.23 us (6%)
    pallas_call x1, Pallas kernels, body(): pl.pallas_call(functools.partial(kernel, n, ng), out_shape=(faces, faces)...  120 us
    unnamed x5, local copies, waits for them, and re-layouts  3.25 us

profile of v1, /device:TPU:0, one launch (start us, length us, event | category | flops | bytes accessed | tf_op | source)
XLA Modules:
  0.0 128.2 jit_solution(447083904320582572)
XLA Ops:
  0.6 0.0 copy-start
  0.6 2.1 %reshape_squeeze.3 = f32[2,12,4,8,2,12]{5,4,3,2,1,0:T(2,128)S(1)} reshape(f32[1,2,12,4,192]{4,3,2,1,0:T(4,128)} %param.11) | data formatting | bytes 147456 | tf_op jit(solution)/shard_map/reshape;squeeze | solution.py:352
  2.8 0.1 copy.13
  2.9 0.1 pad.9
  3.0 1.1 reshape.7.cinv
  4.0 0.0 copy-done
  4.0 0.6 pad.8.cmap
  4.7 120.3 %shard_map.86 = (f32[2,2,48,256]{3,2,1,0:T(8,128)}, f32[2,2,48,256]{3,2,1,0:T(8,128)}) custom-call(f32[2,2,48,256]{3,2,1,0:T(8,128)} %bitcast.21, bf16[2,1024,1024]{2,1,0:T(8,128)(2,1)} %bitcast.15, bf16[2,1024,1024]{2,1,0:T(8,128)(2,1)} %bitcast.16, bf16[2,16,1024]{2,1,0:T(8,128)(2,1)} %pad.8.cmap, f32[4,2,16,256]{3,2,1,0:T(8,128)} %reshape.7.cinv, ...), custom_call_target="tpu_custom_call" | custom-call | tf_op jit(solution)/shard_map/pallas_call | solution.py:363
  125.0 1.6 %copy.17 = f32[1,2,2,48,256]{4,3,2,1,0:T(8,128)} copy(f32[1,2,2,48,256]{4,3,2,1,0:T(8,128)} %bitcast.20) | data formatting | bytes 393216
  126.6 1.6 %copy.18 = f32[1,2,2,48,256]{4,3,2,1,0:T(8,128)} copy(f32[1,2,2,48,256]{4,3,2,1,0:T(8,128)} %bitcast.19) | data formatting | bytes 393216
  (1 shorter events, 0.0 us)
Async XLA Ops:
  0.6 3.4 %copy-start = (bf16[1,2,12,1024]{3,1,2,0:T(2,128)(2,1)S(1)}, bf16[1,2,12,1024]{3,1,2,0:T(2,128)(2,1)}, u32[]{:S(2)}) copy-start(bf16[1,2,12,1024]{3,1,2,0:T(2,128)(2,1)} %param.10) | copy-start | bytes 147460

commit v2 on v1

--- a/solution.py
+++ b/solution.py
@@ -13,6 +13,7 @@
 ITERS = 3
 ORDER = 1024
 PADQ = 16
+TILE = 512
 HALF = 64
 LANES = 128
 HIGHEST = lax.Precision.HIGHEST
@@ -57,10 +58,18 @@
     row = lax.broadcasted_iota(jnp.int32, (LOADS, LANES), 0)
     symmetric = 0.5 * (matrix + transposed(matrix))
     both = jnp.where(lane < HALF, symmetric, pltpu.roll(right, HALF, 1))
-    for k in range(LOADS):
-        pivot_row = both[k : k + 1, :]
-        scaled = pivot_row * (1.0 / both[k : k + 1, k : k + 1])
-        both = jnp.where(row == k, scaled, both - both[:, k : k + 1] * scaled)
+    for k in range(0, LOADS, 2):
+        upper, lower = both[k : k + 1, :], both[k + 1 : k + 2, :]
+        first, second = both[:, k : k + 1], both[:, k + 1 : k + 2]
+        inverse = 1.0 / both[k : k + 1, k : k + 1]
+        beside = both[k : k + 1, k + 1 : k + 2] * inverse
+        under = both[k + 1 : k + 2, k : k + 1]
+        pivot = both[k + 1 : k + 2, k + 1 : k + 2] - under * beside
+        upper = upper * inverse
+        lower = (lower - under * upper) * (1.0 / pivot)
+        rest = both - first * upper - (second - first * beside) * lower
+        upper = upper - beside * lower
+        both = jnp.where(row == k, upper, jnp.where(row == k + 1, lower, rest))
     return pltpu.roll(both, HALF, 1)
 
 
@@ -184,7 +193,11 @@
             ).start()
             return carry
 
-        lax.fori_loop(1, n, step, 0)
+        if n <= 8:
+            for i in range(1, n):
+                step(i, 0)
+        else:
+            lax.fori_loop(1, n, step, 0)
         whole = pltpu.make_async_remote_copy(
             src_ref=buffer.at[r, pl.ds(0, n - 1)], dst_ref=buffer.at[r, pl.ds(0, n - 1)],
             send_sem=ss.at[r], recv_sem=rs.at[r],
@@ -234,19 +247,19 @@
         k = index % 2
         loaded[index].wait()
 
-        @pl.loop(0, ORDER // FACE)
+        @pl.loop(0, ORDER // TILE)
         def _(i):
-            at = pl.multiple_of(i * FACE, FACE)
-            tmat[pl.ds(at, FACE)] = dot_nn(amat[index, pl.ds(at, FACE)], pt[k]).astype(BF16)
-
-        @pl.loop(0, ORDER // FACE)
+            at = pl.multiple_of(i * TILE, TILE)
+            tmat[pl.ds(at, TILE)] = dot_nn(amat[index, pl.ds(at, TILE)], pt[k]).astype(BF16)
+
+        @pl.loop(0, ORDER // TILE)
         def _(i):
-            at = pl.multiple_of(i * FACE, FACE)
-            block = pcol[k, pl.ds(at, FACE)]
+            at = pl.multiple_of(i * TILE, TILE)
+            block = pcol[k, pl.ds(at, TILE)]
             wide = jnp.concatenate([block] * (ORDER // LANES), axis=1)
-            index_of = lax.broadcasted_iota(jnp.int32, (FACE, ORDER), 1)
+            index_of = lax.broadcasted_iota(jnp.int32, (TILE, ORDER), 1)
             pick = jnp.where(index_of == wide, 1.0, 0.0).astype(BF16)
-            qmat[index, pl.ds(at, FACE)] = dot_nn(pick, tmat[...]).astype(BF16)
+            qmat[index, pl.ds(at, TILE)] = dot_nn(pick, tmat[...]).astype(BF16)
 
     def apply(base, rounded):
         return [
@@ -262,9 +275,9 @@
     def precondition(r, count):
         values = apply(0, resid[...].astype(BF16))
         store_field(r, values)
-        halo = halo_start(r)
         gram = dot_nt(jnp.concatenate(values, axis=1), resid[...], HIGHEST)
-        return halo, reduce_start(count, gram)
+        stage = reduce_start(count, gram)
+        return halo_start(r), stage
 
     halo, stage = precondition(1, 0)
     for k in range(2):
@@ -309,9 +322,9 @@
             values[k] + dot_nn(solved[k * HALF : k * HALF + LOADS], basis[k]) for k in range(2)
         ]
         store_field(r, values)
-        halo = halo_start(r)
         gram = dot_nt(direc[...], jnp.concatenate(values, axis=1), HIGHEST)
         stage = reduce_start(count, gram)
+        halo = halo_start(r)
         stage = reduce_middle(count, stage)
         image = jumps(r, halo)
         curvature = reduce_end(count, stage)

time: 128 us -> 147 us (1.15)
  Pallas kernels: 120 us -> 139 us
    pallas_call x1, Pallas kernels: 120 us -> 139 us  [body(): pl.pallas_call(functools.partial(kernel, n, ng), out_shape=(faces, faces)...]
where the time goes in v2:
time: 147 us
  Pallas kernels  139 us (95%)
  local copies, waits for them, and re-layouts  7.23 us (5%)
    pallas_call x1, Pallas kernels, body(): pl.pallas_call(functools.partial(kernel, n, ng), out_shape=(faces, faces)...  139 us
    unnamed x5, local copies, waits for them, and re-layouts  3.25 us

profile of v2, /device:TPU:0, one launch (start us, length us, event | category | flops | bytes accessed | tf_op | source)
XLA Modules:
  0.0 146.7 jit_solution(15973926901548717473)
XLA Ops:
  0.6 0.0 copy-start
  0.6 2.1 %reshape_squeeze.3 = f32[2,12,4,8,2,12]{5,4,3,2,1,0:T(2,128)S(1)} reshape(f32[1,2,12,4,192]{4,3,2,1,0:T(4,128)} %param.11) | data formatting | bytes 147456 | tf_op jit(solution)/shard_map/reshape;squeeze | solution.py:365
  2.8 0.1 copy.13
  2.9 0.1 pad.9
  3.0 1.1 reshape.7.cinv
  4.0 0.0 copy-done
  4.0 0.6 pad.8.cmap
  4.7 138.8 %shard_map.86 = (f32[2,2,48,256]{3,2,1,0:T(8,128)}, f32[2,2,48,256]{3,2,1,0:T(8,128)}) custom-call(f32[2,2,48,256]{3,2,1,0:T(8,128)} %bitcast.21, bf16[2,1024,1024]{2,1,0:T(8,128)(2,1)} %bitcast.15, bf16[2,1024,1024]{2,1,0:T(8,128)(2,1)} %bitcast.16, bf16[2,16,1024]{2,1,0:T(8,128)(2,1)} %pad.8.cmap, f32[4,2,16,256]{3,2,1,0:T(8,128)} %reshape.7.cinv, ...), custom_call_target="tpu_custom_call" | custom-call | tf_op jit(solution)/shard_map/pallas_call | solution.py:376
  143.5 1.6 %copy.17 = f32[1,2,2,48,256]{4,3,2,1,0:T(8,128)} copy(f32[1,2,2,48,256]{4,3,2,1,0:T(8,128)} %bitcast.20) | data formatting | bytes 393216
  145.1 1.6 %copy.18 = f32[1,2,2,48,256]{4,3,2,1,0:T(8,128)} copy(f32[1,2,2,48,256]{4,3,2,1,0:T(8,128)} %bitcast.19) | data formatting | bytes 393216
  (1 shorter events, 0.0 us)
Async XLA Ops:
  0.6 3.4 %copy-start = (bf16[1,2,12,1024]{3,1,2,0:T(2,128)(2,1)S(1)}, bf16[1,2,12,1024]{3,1,2,0:T(2,128)(2,1)}, u32[]{:S(2)}) copy-start(bf16[1,2,12,1024]{3,1,2,0:T(2,128)(2,1)} %param.10) | copy-start | bytes 147460
